TPU v7x, 512 devices: a whole 4x4x16 slice. The times are simulated.
512 devices in a mesh: segment: 4 (over x_hi, core), dp: 128 (over z, y, x_lo).
Axes of the slice: x: 4 (x_hi: 2, x_lo: 2; x = x_hi * 2 + x_lo), y: 4, z: 16, core: 2. Of those that a mesh axis runs over, the one named last changes fastest.
Arguments:
- inputs: bfloat16 [4, 128, 4, 16, 256], P(None, 'dp'), may hold values from -6 to 6
- out_grad: bfloat16 [4, 128, 4, 16, 256], P(None, 'dp'), may hold values from -6 to 6
- w_in: bfloat16 [4, 256, 1024], P('segment'), may hold values from -0.375 to 0.375
- w_out: bfloat16 [4, 1024, 256], P('segment'), may hold values from -0.1875 to 0.1875
- vector_params: float32 [4, 58, 256], P('segment'), may hold values from -2 to 2, as said below
Outputs:
- input_grads: bfloat16 [4, 4, 128, 4, 16, 256], P('segment', None, 'dp')
- step_w_in: float32 [4, 256, 1024], P('segment')
- step_w_out: float32 [4, 1024, 256], P('segment')
- step_vectors: float32 [4, 58, 256], P('segment')
Inputs may be any that keep to these rules, and one draw needn't show every extreme that they name: `vector_params`: rows 0 to 48 are taps of order 0.2, row 50 lies in 0.5 to 1.5, row 53 in 0.2 to 1, the other rows are biases of order 0.5.
All inputs are finite; a program needn't handle non-finite values.
Results may differ from a plain program's by a relative error of at most 0.0095.
Values may be sent and summed in bfloat16 or wider, within the bound.
A program may use at most 128 MiB of HBM per device.

v0:
```python
import functools

import jax
import jax.numpy as jnp
from jax import lax
from jax.experimental import pallas as pl
from jax.experimental.pallas import tpu as pltpu
from jax.sharding import Mesh
from jax.sharding import PartitionSpec as P

F32 = jnp.float32
BF16 = jnp.bfloat16
VTILE = 16
VPAD = 64


def dot(a, b):
    return jnp.dot(a, b, preferred_element_type=F32)


def dot_nt(a, b):
    return lax.dot_general(a, b, (((1,), (1,)), ((), ())), preferred_element_type=F32)


def dot_tn(a, b):
    return lax.dot_general(a, b, (((0,), (0,)), ((), ())), preferred_element_type=F32)


def over_rows(a):
    return jnp.sum(a, axis=0, keepdims=True)


def relay_kernel(
    dims, x_ref, g_ref, win_ref, wout_ref, vec_ref, gath_ref, fac_ref, ig_ref,
    win, wout, vec, X, G, xpad, cv, XH, RSTD, NB, ACT, SL, PJ,
    PIN, POUT, GV, RIN, ROUT, RV, IG, S, RB, ZB, VZ, GATH, SQ,
    load_sem, wsend, wrecv, hsend, hrecv, isend, irecv, csend, crecv,
    psend, precv, zsend, zrecv, vsend, vrecv, bsend, brecv, asend, arecv, gsend, grecv,
    qsend, qrecv,
):
    nz, ny, nx, params = dims
    nplane = ny * nx
    core = lax.axis_index("core")
    sx = lax.axis_index("sx")
    z = lax.axis_index("z")
    y = lax.axis_index("y")
    xl = lax.axis_index("xl")
    plane = y * nx + xl
    pair, height, width, chans = X.shape[1:]
    rows = pair * height * width
    hidden = win.shape[2]
    quarters = hidden // chans
    in_rows = chans // nplane
    out_rows = hidden // nplane
    part = in_rows * quarters + out_rows
    zrows = part // nz
    vlanes = VPAD * chans // nplane // VTILE
    vcols = chans // vlanes
    owner = lax.rem(2 * plane + core, nz)

    def copy(src, dst, ss, rs, dev):
        return pltpu.make_async_remote_copy(
            src_ref=src, dst_ref=dst, send_sem=ss, recv_sem=rs,
            device_id=dev, device_id_type=pl.DeviceIdType.MESH,
        )

    sib = {"core": 1 - core}
    far = {"sx": 1 - sx}
    diag = {"core": 1 - core, "sx": 1 - sx}

    def plane_dev(r):
        q = lax.rem(plane + r, nplane)
        return q, {"y": q // nx, "xl": lax.rem(q, nx)}

    def z_dev(r):
        q = lax.rem(z + r, nz)
        return q, {"z": q}

    loads = [
        pltpu.make_async_copy(vec_ref, vec.at[core], load_sem.at[0]),
        pltpu.make_async_copy(win_ref, win.at[core], load_sem.at[1]),
        pltpu.make_async_copy(wout_ref, wout.at[core], load_sem.at[2]),
    ]
    for c in loads:
        c.start()

    barrier = pltpu.get_barrier_semaphore()

    def hello(dev):
        pl.semaphore_signal(barrier, inc=1, device_id=dev, device_id_type=pl.DeviceIdType.MESH)

    hello(sib)
    hello(far)
    hello(diag)

    @pl.loop(1, nplane)
    def _(r):
        hello(plane_dev(r)[1])

    @pl.loop(1, nz)
    def _(r):
        hello(z_dev(r)[1])

    zero_side = jnp.zeros((pair, height, 8, chans), F32)
    xpad[:, :, 0:8, :] = zero_side
    xpad[:, :, 8 + width : 16 + width, :] = zero_side
    GV[...] = jnp.zeros(GV.shape, F32)
    GATH[plane, part:, :] = jnp.zeros((VTILE, chans), BF16)

    @pl.when(sx == 0)
    def _():
        X[0] = x_ref[pl.ds(core * pair, pair)]

    @pl.when(sx == 1)
    def _():
        G[2] = g_ref[pl.ds(core * pair, pair)]

    pl.semaphore_wait(barrier, 3 + (nplane - 1) + (nz - 1))

    wcopies = [
        copy(vec_ref, vec.at[core], wsend.at[0], wrecv.at[0], sib),
        copy(win_ref, win.at[core], wsend.at[1], wrecv.at[1], sib),
        copy(wout_ref, wout.at[core], wsend.at[2], wrecv.at[2], sib),
    ]
    for c in wcopies:
        c.start()

    def hop_x():
        return copy(X.at[2], X.at[0], hsend, hrecv, far)

    def hop_g():
        return copy(G.at[0], G.at[2], hsend, hrecv, far)

    @pl.when(sx == 1)
    def _():
        hop_x().wait_recv()

    def row(k, t):
        return vec[k, t : t + 1, :]

    def forward(k, carry):
        @pl.when(core == k)
        def _():
            for c in loads:
                c.wait()

        @pl.when(core != k)
        def _():
            for c in wcopies:
                c.wait_recv()

        xpad[:, :, 8 : 8 + width, :] = X[k].astype(F32)
        for half in range(chans // 128):
            lanes = slice(half * 128, half * 128 + 128)
            acc = [None] * height
            for j in range(7):
                shifted = [xpad[:, h, 5 + j : 5 + j + width, lanes] for h in range(height)]
                for i in range(7):
                    tap = vec[k, 7 * i + j : 7 * i + j + 1, lanes][None]
                    for h in range(height):
                        if 0 <= h + i - 3 < height:
                            term = shifted[h + i - 3] * tap
                            acc[h] = term if acc[h] is None else acc[h] + term
            bias = vec[k, 49:50, lanes][None]
            for h in range(height):
                cv[:, h, :, lanes] = acc[h] + bias
        conv = cv[...].reshape(rows, chans)
        mean = jnp.sum(conv, axis=1, keepdims=True) * (1.0 / chans)
        centered = conv - mean
        var = jnp.sum(centered * centered, axis=1, keepdims=True) * (1.0 / chans)
        rstd = lax.rsqrt(var + 1e-06)
        xhat = centered * rstd
        XH[k] = xhat
        RSTD[k] = jnp.broadcast_to(rstd, (rows, 128))
        normed = (xhat * row(k, 50) + row(k, 51)).astype(BF16)
        NB[k] = normed
        proj = jnp.zeros((rows, chans), F32)
        for q in range(quarters):
            cols = slice(q * chans, (q + 1) * chans)
            pre = dot(normed, win[k, :, cols]) + row(k, 54 + q)
            cumulative = 0.5 * (1.0 + lax.erf(pre * 0.7071067811865476))
            act = (pre * cumulative).astype(BF16)
            ACT[k, :, cols] = act
            SL[k, :, cols] = cumulative + pre * jnp.exp(-0.5 * pre * pre) * 0.3989422804014327
            proj = proj + dot(act, wout[k, cols, :])
        proj = proj + row(k, 52)
        PJ[k] = proj
        out = X[k].astype(F32).reshape(rows, chans) + row(k, 53) * proj
        X[k + 1] = out.astype(BF16).reshape(pair, height, width, chans)
        return carry

    lax.fori_loop(0, 2, forward, 0)

    @pl.when(sx == 0)
    def _():
        hop_x().start()
        hop_g().wait_recv()

    def grad_copies(k):
        return [
            copy(POUT.at[k], ROUT, csend.at[0], crecv.at[0], sib),
            copy(PIN.at[k], RIN, csend.at[1], crecv.at[1], sib),
            copy(GV.at[k], RV, csend.at[2], crecv.at[2], sib),
        ]

    def ig_copy(k):
        return copy(G.at[k], IG.at[pl.ds(core * pair, pair)], isend, irecv, sib)

    def plane_copy(r):
        q, dev = plane_dev(r)
        return copy(S.at[q], RB.at[r], psend.at[r], precv.at[r], dev)

    def chip_sum(k):
        for c in grad_copies(k):
            c.wait_recv()

        for t in range(nplane):
            at_row, at_col = (t // vcols) * VTILE, (t % vcols) * vlanes
            tile = (slice(at_row, at_row + VTILE), slice(at_col, at_col + vlanes))
            S[t, part:, :] = jnp.zeros((VTILE, chans), BF16)
            S[t, part:, 0:vlanes] = (GV[(k,) + tile] + RV[tile]).astype(BF16)

        @pl.loop(1, nplane + 1)
        def _(r):
            q = lax.rem(plane + r, nplane)
            at = pl.ds(pl.multiple_of(q * in_rows, in_rows), in_rows)
            for t in range(quarters):
                cols = slice(t * chans, (t + 1) * chans)
                S[q, t * in_rows : (t + 1) * in_rows, :] = (
                    PIN[k, at, cols].astype(F32) + RIN[at, cols].astype(F32)
                ).astype(BF16)
            at = pl.ds(pl.multiple_of(q * out_rows, out_rows), out_rows)
            S[q, quarters * in_rows : part, :] = (
                POUT[k, at, :].astype(F32) + ROUT[at, :].astype(F32)
            ).astype(BF16)

            @pl.when(r < nplane)
            def _():
                plane_copy(r).start()

    def backward(step, carry):
        k = 1 - step
        gf = G[k + 1].astype(F32).reshape(rows, chans)
        GV[k, 53:54, :] = over_rows(gf * PJ[k])
        dproj = gf * row(k, 53)
        GV[k, 52:53, :] = over_rows(dproj)
        dproj_b = dproj.astype(BF16)
        normed = NB[k]
        dn = jnp.zeros((rows, chans), F32)
        for q in range(quarters):
            cols = slice(q * chans, (q + 1) * chans)
            dact = dot_nt(dproj_b, wout[k, cols, :])
            POUT[k, cols, :] = dot_tn(ACT[k, :, cols], dproj_b).astype(BF16)
            dpre = dact * SL[k, :, cols]
            GV[k, 54 + q : 55 + q, :] = over_rows(dpre)
            dpre_b = dpre.astype(BF16)
            PIN[k, :, cols] = dot_tn(normed, dpre_b).astype(BF16)
            dn = dn + dot_nt(dpre_b, win[k, :, cols])

        @pl.when(core != k)
        def _():
            for c in grad_copies(k)[:2]:
                c.start()

        @pl.when((core == 1) & (k == 0))
        def _():
            chip_sum(1)

        xhat = XH[k]
        GV[k, 50:51, :] = over_rows(dn * xhat)
        GV[k, 51:52, :] = over_rows(dn)
        dxh = dn * row(k, 50)
        m1 = jnp.sum(dxh, axis=1, keepdims=True) * (1.0 / chans)
        m2 = jnp.sum(dxh * xhat, axis=1, keepdims=True) * (1.0 / chans)
        rstd = RSTD[k][:, 0:1]
        dconv = (dxh - m1 - xhat * m2) * rstd
        GV[k, 49:50, :] = over_rows(dconv)
        xpad[:, :, 8 : 8 + width, :] = dconv.reshape(pair, height, width, chans)
        for half in range(chans // 128):
            lanes = slice(half * 128, half * 128 + 128)
            acc = [G[k + 1, :, h, :, lanes].astype(F32) for h in range(height)]
            xs = [X[k, :, h, :, lanes].astype(F32) for h in range(height)]
            for j in range(7):
                shifted = [xpad[:, h, 11 - j : 11 - j + width, lanes] for h in range(height)]
                for i in range(7):
                    t = 7 * i + j
                    tap = vec[k, t : t + 1, lanes][None]
                    total = None
                    for h in range(height):
                        if 0 <= h - i + 3 < height:
                            acc[h] = acc[h] + shifted[h - i + 3] * tap
                            term = xs[h] * shifted[h - i + 3]
                            total = term if total is None else total + term
                    GV[k, t : t + 1, lanes] = over_rows(total.reshape(pair * width, 128))
            for h in range(height):
                G[k, :, h, :, lanes] = acc[h].astype(BF16)

        @pl.when(core != k)
        def _():
            grad_copies(k)[2].start()
            ig_copy(k).start()

        @pl.when(core == k)
        def _():
            IG[pl.ds(core * pair, pair)] = G[k]

        return carry

    lax.fori_loop(0, 2, backward, 0)

    @pl.when(sx == 1)
    def _():
        hop_g().start()

    @pl.when(core == 0)
    def _():
        chip_sum(0)

    def z_copy(r):
        q, dev = z_dev(r)
        src = S.at[plane, pl.ds(pl.multiple_of(q * zrows, zrows), zrows)]
        return copy(src, ZB.at[r], zsend.at[r], zrecv.at[r], dev)

    @pl.loop(1, nplane)
    def _(r):
        plane_copy(r).wait_recv()

    def vec_up():
        r = lax.rem(owner - z + nz, nz)
        src = S.at[plane, pl.ds(part, VTILE), pl.ds(0, vlanes)]
        return copy(src, VZ.at[r], vsend, vrecv.at[r], {"z": owner})

    vacc = S[plane, part:, 0:vlanes].astype(F32)
    for r in range(1, nplane):
        vacc = vacc + RB[r, part:, 0:vlanes].astype(F32)
    S[plane, part:, 0:vlanes] = vacc.astype(BF16)

    @pl.when(z != owner)
    def _():
        vec_up().start()

    @pl.loop(1, nz + 1)
    def _(r):
        q = lax.rem(z + r, nz)
        at = pl.ds(pl.multiple_of(q * zrows, zrows), zrows)
        acc = S[plane, at, :].astype(F32)
        for t in range(1, nplane):
            acc = acc + RB[t, at, :].astype(F32)
        S[plane, at, :] = acc.astype(BF16)

        @pl.when(r < nz)
        def _():
            z_copy(r).start()

    mine = pl.ds(pl.multiple_of(z * zrows, zrows), zrows)

    def share_copy(r):
        _, dev = z_dev(r)
        return copy(GATH.at[plane, mine], GATH.at[plane, mine], asend.at[r], arecv.at[r], dev)

    @pl.loop(1, nz)
    def _(r):
        z_copy(r).wait_recv()

    acc = S[plane, mine, :].astype(F32)
    for r in range(1, nz):
        acc = acc + ZB[r].astype(F32)
    GATH[plane, mine, :] = acc.astype(BF16)

    @pl.loop(1, nz)
    def _(r):
        share_copy(r).start()

    vtile = (plane, pl.ds(part, VTILE), pl.ds(0, vlanes))

    def vec_down(r):
        _, dev = z_dev(r)
        return copy(GATH.at[vtile], GATH.at[vtile], bsend.at[r], brecv, dev)

    @pl.when(z == owner)
    def _():
        @pl.loop(1, nz)
        def _(r):
            copy(VZ.at[r], VZ.at[r], vsend, vrecv.at[r], {"z": owner}).wait_recv()

        total = S[plane, part:, 0:vlanes].astype(F32)
        for r in range(1, nz):
            total = total + VZ[r].astype(F32)
        GATH[plane, part:, 0:vlanes] = total.astype(BF16)

        @pl.loop(1, nz)
        def _(r):
            vec_down(r).start()

    @pl.when(z != owner)
    def _():
        vec_down(1).wait_recv()

    @pl.loop(1, nz)
    def _(r):
        q = lax.rem(z - r + nz, nz)
        theirs = pl.ds(pl.multiple_of(q * zrows, zrows), zrows)
        copy(
            GATH.at[plane, theirs], GATH.at[plane, theirs], asend.at[r], arecv.at[r], {"z": q}
        ).wait_recv()

    def whole_copy(r):
        _, dev = plane_dev(r)
        return copy(GATH.at[plane], GATH.at[plane], gsend.at[r], grecv.at[r], dev)

    @pl.loop(1, nplane)
    def _(r):
        whole_copy(r).start()

    @pl.loop(1, nplane)
    def _(r):
        q = lax.rem(plane - r + nplane, nplane)
        copy(GATH.at[q], GATH.at[q], gsend.at[r], grecv.at[r], plane_dev(r)[1]).wait_recv()

    def squares(q, carry):
        a, b = carry
        v = GATH[q, 0:part, :].astype(F32)
        u = GATH[q, part:, 0:vlanes].astype(F32)
        return (
            a + jnp.sum((v * v).reshape(part // 8, 8, chans), axis=0),
            b + jnp.sum((u * u).reshape(VTILE // 8, 8, vlanes), axis=0),
        )

    a, b = lax.fori_loop(
        0, nplane, squares, (jnp.zeros((8, chans), F32), jnp.zeros((8, vlanes), F32))
    )
    seg = sx * 2 + core
    SQ[seg] = jnp.broadcast_to(jnp.sum(a) + jnp.sum(b), (8, 128))
    mates = [sib, far, diag]
    sq_copies = [
        copy(SQ.at[seg], SQ.at[seg], qsend.at[t], qrecv.at[t], dev) for t, dev in enumerate(mates)
    ]
    for c in sq_copies:
        c.start()
    ig_copy(0).wait_recv()
    ig_ref[...] = IG[...]
    gath_ref[...] = GATH[...]
    mate_seg = [sx * 2 + 1 - core, (1 - sx) * 2 + core, (1 - sx) * 2 + 1 - core]
    for t, dev in enumerate(mates):
        copy(
            SQ.at[mate_seg[t]], SQ.at[mate_seg[t]], qsend.at[t], qrecv.at[t], dev
        ).wait_recv()
    total = (SQ[0] + SQ[1]) + (SQ[2] + SQ[3])
    fac_ref[...] = jnp.minimum(1.0, (params**0.5) * lax.rsqrt(total + 1e-06))

    for c in wcopies:
        c.wait_send()
    hop_x().wait_send()
    ig_copy(0).wait_send()
    for c in grad_copies(0):
        c.wait_send()

    @pl.loop(1, nplane)
    def _(r):
        plane_copy(r).wait_send()
        whole_copy(r).wait_send()

    @pl.loop(1, nz)
    def _(r):
        z_copy(r).wait_send()
        share_copy(r).wait_send()

    @pl.when(z != owner)
    def _():
        vec_up().wait_send()

    @pl.when(z == owner)
    def _():
        @pl.loop(1, nz)
        def _(r):
            vec_down(r).wait_send()

    for c in sq_copies:
        c.wait_send()


def scale_kernel(gath, fac, ig, o_in, o_out, o_vec, o_ig):
    nplane, rows, chans = gath.shape
    part = rows - VTILE
    quarters = o_in.shape[1] // chans
    in_rows = chans // nplane
    out_rows = o_out.shape[0] // nplane
    vlanes = VPAD * chans // nplane // VTILE
    vcols = chans // vlanes
    f = fac[0:1, 0:1]
    for p in range(nplane):
        for q in range(quarters):
            o_in[p * in_rows : (p + 1) * in_rows, q * chans : (q + 1) * chans] = (
                gath[p, q * in_rows : (q + 1) * in_rows, :].astype(F32) * f
            )
        o_out[p * out_rows : (p + 1) * out_rows, :] = gath[p, quarters * in_rows : part, :].astype(F32) * f
        at_row, at_col = (p // vcols) * VTILE, (p % vcols) * vlanes
        size = min(VTILE, o_vec.shape[0] - at_row)
        o_vec[at_row : at_row + size, at_col : at_col + vlanes] = (
            gath[p, part:, 0:vlanes].astype(F32) * f
        )[0:size]
    o_ig[...] = ig[...]


def per_device(dims, inputs, out_grad, w_in, w_out, vector_params):
    nz, ny, nx, params = dims
    nplane = ny * nx
    micros, _, height, width, chans = inputs.shape
    hidden = w_in.shape[2]
    vrows = vector_params.shape[1]
    pair = micros // 2
    rows = pair * height * width
    part = (chans * hidden * 2) // chans // nplane
    zrows = part // nz
    vlanes = VPAD * chans // nplane // VTILE
    maps = (micros, height, width, chans)
    small = (pair, height, width, chans)
    vm = pltpu.VMEM
    dma = pltpu.SemaphoreType.DMA
    in_vmem = pl.BlockSpec(memory_space=pltpu.VMEM)
    anywhere = pl.BlockSpec(memory_space=pl.ANY)
    gath, fac, ig = pl.pallas_call(
        functools.partial(relay_kernel, dims),
        out_shape=(
            jax.ShapeDtypeStruct((nplane, part + VTILE, chans), BF16),
            jax.ShapeDtypeStruct((8, 128), F32),
            jax.ShapeDtypeStruct(maps, BF16),
        ),
        in_specs=[in_vmem, in_vmem, anywhere, anywhere, anywhere],
        out_specs=(in_vmem, in_vmem, in_vmem),
        scratch_shapes=[
            vm((2, chans, hidden), BF16),
            vm((2, hidden, chans), BF16),
            vm((2, vrows, chans), F32),
            vm((3,) + small, BF16),
            vm((3,) + small, BF16),
            vm((pair, height, width + 16, chans), F32),
            vm(small, F32),
            vm((2, rows, chans), F32),
            vm((2, rows, 128), F32),
            vm((2, rows, chans), BF16),
            vm((2, rows, hidden), BF16),
            vm((2, rows, hidden), F32),
            vm((2, rows, chans), F32),
            vm((2, chans, hidden), BF16),
            vm((2, hidden, chans), BF16),
            vm((2, VPAD, chans), F32),
            vm((chans, hidden), BF16),
            vm((hidden, chans), BF16),
            vm((VPAD, chans), F32),
            vm(maps, BF16),
            vm((nplane, part + VTILE, chans), BF16),
            vm((nplane, part + VTILE, chans), BF16),
            vm((nz, zrows, chans), BF16),
            vm((nz, VTILE, vlanes), BF16),
            vm((nplane, part + VTILE, chans), BF16),
            vm((4, 8, 128), F32),
            dma((3,)),
            dma((3,)), dma((3,)),
            dma, dma,
            dma, dma,
            dma((3,)), dma((3,)),
            dma((nplane,)), dma((nplane,)),
            dma((nz,)), dma((nz,)),
            dma, dma((nz,)),
            dma((nz,)), dma,
            dma((nz,)), dma((nz,)),
            dma((nplane,)), dma((nplane,)),
            dma((3,)), dma((3,)),
        ],
        compiler_params=pltpu.CompilerParams(
            collective_id=0, has_side_effects=True, vmem_limit_bytes=40 * 1024 * 1024
        ),
        name="relay",
    )(
        inputs.reshape(maps), out_grad.reshape(maps), w_in[0], w_out[0], vector_params[0]
    )
    o_in, o_out, o_vec, o_ig = pl.pallas_call(
        scale_kernel,
        out_shape=(
            jax.ShapeDtypeStruct((chans, hidden), F32),
            jax.ShapeDtypeStruct((hidden, chans), F32),
            jax.ShapeDtypeStruct((vrows, chans), F32),
            jax.ShapeDtypeStruct(maps, BF16),
        ),
        in_specs=[in_vmem] * 3,
        out_specs=(in_vmem,) * 4,
        compiler_params=pltpu.CompilerParams(vmem_limit_bytes=24 * 1024 * 1024),
        name="scale",
    )(gath, fac, ig)
    return (
        o_ig.reshape((1, micros, 1, height, width, chans)), o_in[None], o_out[None], o_vec[None]
    )


def solution(mesh):
    nx = 2
    ny = 4
    nz = mesh.shape["dp"] // (nx * ny)
    return program_on(mesh, nz, ny, nx)


def program_on(mesh, nz, ny, nx, params=2156544):
    split = Mesh(mesh.devices.reshape(2, 2, nz, ny, nx), ("sx", "core", "z", "y", "xl"))
    dp = ("z", "y", "xl")
    seg = ("sx", "core")
    in_specs = (
        P(None, dp, None, None, None),
        P(None, dp, None, None, None),
        P(seg, None, None),
        P(seg, None, None),
        P(seg, None, None),
    )
    out_specs = (
        P(seg, None, dp, None, None, None),
        P(seg, None, None),
        P(seg, None, None),
        P(seg, None, None),
    )
    return jax.shard_map(
        functools.partial(per_device, (nz, ny, nx, params)),
        mesh=split, in_specs=in_specs, out_specs=out_specs, check_vma=False,
    )
```

profile of v0, /device:TPU:6, one launch (start us, length us, event | category | flops | bytes accessed | tf_op | source)
XLA Modules:
  0.0 103.8 jit_solution(6895931264006324438)
XLA Ops:
  0.6 0.8 copy.13
  1.5 0.0 copy-start
  1.5 1.0 %copy-done = bf16[1,256,1024]{2,1,0:T(8,128)(2,1)S(1)} copy-done((bf16[1,256,1024]{2,1,0:T(8,128)(2,1)S(1)}, bf16[1,256,1024]{2,1,0:T(8,128)(2,1)}, u32[]{:S(2)}) %copy-start) | copy-done | bytes 524312
  2.5 0.0 copy-start.1
  2.5 1.0 %copy-done.1 = bf16[1,1024,256]{2,1,0:T(8,128)(2,1)S(1)} copy-done((bf16[1,1024,256]{2,1,0:T(8,128)(2,1)S(1)}, bf16[1,1024,256]{2,1,0:T(8,128)(2,1)}, u32[]{:S(2)}) %copy-start.1) | copy-done | bytes 524312
  3.5 0.0 copy-start.2
  3.5 0.9 copy-done.2
  4.5 0.0 copy-start.3
  4.5 0.9 copy-done.3
  5.4 96.2 %relay.1 = (bf16[8,272,256]{2,1,0:T(8,128)(2,1)S(1)}, f32[8,128]{1,0:T(8,128)S(1)}, bf16[4,4,16,256]{3,2,1,0:T(8,128)(2,1)S(1)}) custom-call(bf16[4,4,16,256]{3,2,1,0:T(8,128)(2,1)S(1)} %bitcast.16, bf16[4,4,16,256]{3,2,1,0:T(8,128)(2,1)S(1)} %bitcast.17, bf16[256,1024]{1,0:T(8,128)(2,1)S(1)} %bitcast.13, bf16[1024,256]{1,0:T(8,128)(2,1)S(1)} %bitcast.14, ...), custom_call_target="tpu_custom_call" | custom-call | tf_op jit(solution)/shard_map/relay/pallas_call | solution.py:522
  101.6 1.5 %scale.1 = (f32[256,1024]{1,0:T(8,128)}, f32[1024,256]{1,0:T(8,128)}, f32[58,256]{1,0:T(8,128)S(1)}, bf16[4,4,16,256]{3,2,1,0:T(8,128)(2,1)}) custom-call(bf16[8,272,256]{2,1,0:T(8,128)(2,1)S(1)} %get-tuple-element.11.gath, f32[8,128]{1,0:T(8,128)S(1)} %get-tuple-element.12.fac, bf16[4,4,16,256]{3,2,1,0:T(8,128)(2,1)S(1)} %get-tuple-element.13.ig), custom_call_target="tpu_custom_call" | custom-call | tf_op jit(solution)/shard_map/scale/pallas_call | solution.py:578
  103.1 0.7 copy.10
Async XLA Ops:
  1.5 1.0 %copy-start = (bf16[1,256,1024]{2,1,0:T(8,128)(2,1)S(1)}, bf16[1,256,1024]{2,1,0:T(8,128)(2,1)}, u32[]{:S(2)}) copy-start(bf16[1,256,1024]{2,1,0:T(8,128)(2,1)} %param.7) | copy-start | bytes 1572868
  2.5 1.0 %copy-start.1 = (bf16[1,1024,256]{2,1,0:T(8,128)(2,1)S(1)}, bf16[1,1024,256]{2,1,0:T(8,128)(2,1)}, u32[]{:S(2)}) copy-start(bf16[1,1024,256]{2,1,0:T(8,128)(2,1)} %param.8) | copy-start | bytes 1572868
  3.5 0.9 copy-start.2
  4.5 0.9 copy-start.3
where the time goes:
time: 104 us
  Pallas kernels  97.7 us (94%)
  local copies, waits for them, and re-layouts  5.41 us (5%)
    pallas_call x1, Pallas kernels, per_device(): pl.pallas_call(functools.partial(relay_kernel, dims), out_shape=(jax.Shap...  96.2 us
    unnamed x10, local copies, waits for them, and re-layouts  5.41 us

commit v1 on v0

v1 whole, which is shorter than its diff:
```python
import functools

import jax
import jax.numpy as jnp
from jax import lax
from jax.experimental import pallas as pl
from jax.experimental.pallas import tpu as pltpu
from jax.sharding import Mesh
from jax.sharding import PartitionSpec as P

F32 = jnp.float32
BF16 = jnp.bfloat16
VTILE = 16
VPAD = 64


def dot(a, b):
    return jnp.dot(a, b, preferred_element_type=F32)


def dot_nt(a, b):
    return lax.dot_general(a, b, (((1,), (1,)), ((), ())), preferred_element_type=F32)


def dot_tn(a, b):
    return lax.dot_general(a, b, (((0,), (0,)), ((), ())), preferred_element_type=F32)


def over_rows(a):
    return jnp.sum(a, axis=0, keepdims=True)


def spans(nz):
    if nz == 16:
        return ((11, 16), (6, 11), (0, 6)), ((0, 1), (1, 5), (5, 9), (9, 13), (13, 16))
    return ((1, nz), (0, 1)), ((0, 1), (1, nz))


def offset(s):
    return (s + 1) // 2 if s % 2 else -(s // 2)


def mirror(s, nz):
    if s == 0 or s == nz - 1:
        return s
    return s + 1 if s % 2 else s - 1


def relay_kernel(
    dims, x_ref, g_ref, win_ref, wout_ref, vec_ref, gath_ref, gathv_ref, fac_ref, ig_ref,
    win, wout, vec, X, G, xpad, cv, XH, RSTD, NB, ACT, SL, PJ,
    PG, GV, RG, RV, IG, S, RB, SV, RBV, ZB, VZ, GATH, GATHV, SQS, SQZ, SQP,
    load_sem, wsend, wrecv, hsend, hrecv, isend, irecv, csend, crecv, cvsend, cvrecv,
    psend, precv, pvsend, pvrecv, zsend, zrecv, vsend, vrecv, bsend, brecv, asend, arecv,
    gsend, grecv, gvsend, gvrecv, qsend, qrecv, qzsend, qzrecv, qpsend, qprecv,
):
    nz, ny, nx, params = dims
    nplane = ny * nx
    core = lax.axis_index("core")
    sx = lax.axis_index("sx")
    z = lax.axis_index("z")
    y = lax.axis_index("y")
    xl = lax.axis_index("xl")
    plane = y * nx + xl
    pair, height, width, chans = X.shape[1:]
    rows = pair * height * width
    hidden = win.shape[2]
    quarters = hidden // chans
    part = 2 * hidden // nplane
    zrows = part // nz
    vlanes = SV.shape[2]
    vcols = chans // vlanes
    owner = lax.rem(2 * plane + core, nz)
    chunks, groups = spans(nz)

    def copy(src, dst, ss, rs, dev):
        return pltpu.make_async_remote_copy(
            src_ref=src, dst_ref=dst, send_sem=ss, recv_sem=rs,
            device_id=dev, device_id_type=pl.DeviceIdType.MESH,
        )

    sib = {"core": 1 - core}
    far = {"sx": 1 - sx}
    diag = {"core": 1 - core, "sx": 1 - sx}

    def plane_dev(r):
        q = lax.rem(plane + r, nplane)
        return q, {"y": q // nx, "xl": lax.rem(q, nx)}

    def z_at(by):
        return lax.rem(z + by + nz, nz)

    loads = [
        pltpu.make_async_copy(vec_ref, vec.at[core], load_sem.at[0]),
        pltpu.make_async_copy(win_ref, win.at[core], load_sem.at[1]),
        pltpu.make_async_copy(wout_ref, wout.at[core], load_sem.at[2]),
    ]
    for c in loads:
        c.start()
    my_micros = pl.ds(core * pair, pair)

    def load_x():
        return pltpu.make_async_copy(x_ref.at[my_micros], X.at[0], load_sem.at[3])

    def load_g():
        return pltpu.make_async_copy(g_ref.at[my_micros], G.at[2], load_sem.at[3])

    @pl.when(sx == 0)
    def _():
        load_x().start()

    @pl.when(sx == 1)
    def _():
        load_g().start()

    barrier = pltpu.get_barrier_semaphore()

    def hello(dev):
        pl.semaphore_signal(barrier, inc=1, device_id=dev, device_id_type=pl.DeviceIdType.MESH)

    @pl.loop(1, nz)
    def _(r):
        hello({"z": z_at(r)})

    @pl.loop(1, nplane)
    def _(r):
        hello(plane_dev(r)[1])

    hello(diag)
    hello(far)
    hello(sib)

    zero_side = jnp.zeros((pair, height, 8, chans), F32)
    xpad[:, :, 0:8, :] = zero_side
    xpad[:, :, 8 + width : 16 + width, :] = zero_side
    GV[...] = jnp.zeros(GV.shape, F32)

    @pl.when(sx == 0)
    def _():
        load_x().wait()

    @pl.when(sx == 1)
    def _():
        load_g().wait()

    pl.semaphore_wait(barrier, 3 + (nplane - 1) + (nz - 1))

    wcopies = [
        copy(vec_ref, vec.at[core], wsend.at[0], wrecv.at[0], sib),
        copy(win_ref, win.at[core], wsend.at[1], wrecv.at[1], sib),
        copy(wout_ref, wout.at[core], wsend.at[2], wrecv.at[2], sib),
    ]
    for c in wcopies:
        c.start()

    def hop_x():
        return copy(X.at[2], X.at[0], hsend, hrecv, far)

    def hop_g():
        return copy(G.at[0], G.at[2], hsend, hrecv, far)

    @pl.when(sx == 1)
    def _():
        hop_x().wait_recv()

    def row(k, t):
        return vec[k, t]

    def forward(k, carry):
        @pl.when(core == k)
        def _():
            for c in loads:
                c.wait()

        @pl.when(core != k)
        def _():
            for c in wcopies:
                c.wait_recv()

        xpad[:, :, 8 : 8 + width, :] = X[k].astype(F32)
        for half in range(chans // 128):
            lanes = slice(half * 128, half * 128 + 128)
            acc = [None] * height
            for j in range(7):
                shifted = [xpad[:, h, 5 + j : 5 + j + width, lanes] for h in range(height)]
                for i in range(7):
                    tap = vec[k, 7 * i + j, :, lanes][None]
                    for h in range(height):
                        if 0 <= h + i - 3 < height:
                            term = shifted[h + i - 3] * tap
                            acc[h] = term if acc[h] is None else acc[h] + term
            bias = vec[k, 49, :, lanes][None]
            for h in range(height):
                cv[:, h, :, lanes] = acc[h] + bias
        conv = cv[...].reshape(rows, chans)
        mean = jnp.sum(conv, axis=1, keepdims=True) * (1.0 / chans)
        centered = conv - mean
        var = jnp.sum(centered * centered, axis=1, keepdims=True) * (1.0 / chans)
        rstd = lax.rsqrt(var + 1e-06)
        xhat = centered * rstd
        XH[k] = xhat
        RSTD[k] = jnp.broadcast_to(rstd, (rows, 128))
        normed = (xhat * row(k, 50) + row(k, 51)).astype(BF16)
        NB[k] = normed
        proj = jnp.zeros((rows, chans), F32)
        for q in range(quarters):
            cols = slice(q * chans, (q + 1) * chans)
            pre = dot(normed, win[k, :, cols]) + row(k, 54 + q)
            cumulative = 0.5 * (1.0 + lax.erf(pre * 0.7071067811865476))
            act = (pre * cumulative).astype(BF16)
            ACT[k, :, cols] = act
            SL[k, :, cols] = cumulative + pre * jnp.exp(-0.5 * pre * pre) * 0.3989422804014327
            proj = proj + dot(act, wout[k, cols, :])
        proj = proj + row(k, 52)
        PJ[k] = proj
        out = X[k].astype(F32).reshape(rows, chans) + row(k, 53) * proj
        X[k + 1] = out.astype(BF16).reshape(pair, height, width, chans)
        return carry

    lax.fori_loop(0, 2, forward, 0)

    @pl.when(sx == 0)
    def _():
        hop_x().start()
        hop_g().wait_recv()

    def grad_copy(k, t):
        at = pl.ds(t * chans, chans)
        return copy(PG.at[k, at], RG.at[at], csend.at[t], crecv.at[t], sib)

    def vec_copy(k):
        return copy(GV.at[k], RV, cvsend, cvrecv, sib)

    def ig_copy(k):
        return copy(G.at[k], IG.at[my_micros], isend, irecv, sib)

    def plane_copy(c, r):
        lo, hi = chunks[c]
        q, dev = plane_dev(r)
        at = pl.ds(lo * zrows, (hi - lo) * zrows)
        return copy(S.at[q, at], RB.at[r, at], psend.at[c, r], precv.at[c, r], dev)

    def plane_vec_copy(r):
        q, dev = plane_dev(r)
        return copy(SV.at[q], RBV.at[r], pvsend.at[r], pvrecv.at[r], dev)

    def chip_sum(k):
        for t in range(2 * quarters):
            grad_copy(k, t).wait_recv()
        for c, (lo, hi) in enumerate(chunks):

            @pl.loop(1, nplane + 1)
            def _(r):
                p = lax.rem(plane + r, nplane)
                for s in range(lo, hi):
                    start = p * part + z_at(offset(s)) * zrows
                    at = pl.ds(pl.multiple_of(start, zrows), zrows)
                    S[p, s * zrows : (s + 1) * zrows, :] = (
                        PG[k, at, :].astype(F32) + RG[at, :].astype(F32)
                    ).astype(BF16)

                @pl.when(r < nplane)
                def _():
                    plane_copy(c, r).start()

    def chip_vec_sum(k):
        vec_copy(k).wait_recv()
        for t in range(nplane):
            at_row, at_col = (t // vcols) * VTILE, (t % vcols) * vlanes
            tile = (slice(at_row, at_row + VTILE), slice(at_col, at_col + vlanes))
            SV[t] = (GV[(k,) + tile] + RV[tile]).astype(BF16)

        @pl.loop(1, nplane)
        def _(r):
            plane_vec_copy(r).start()

    def backward(step, carry):
        k = 1 - step
        gf = G[k + 1].astype(F32).reshape(rows, chans)
        GV[k, 53:54, :] = over_rows(gf * PJ[k])
        dproj = gf * row(k, 53)
        GV[k, 52:53, :] = over_rows(dproj)
        dproj_b = dproj.astype(BF16)
        normed = NB[k]
        dn = jnp.zeros((rows, chans), F32)
        for q in range(quarters):
            cols = slice(q * chans, (q + 1) * chans)
            dact = dot_nt(dproj_b, wout[k, cols, :])
            PG[k, hidden + q * chans : hidden + (q + 1) * chans, :] = dot_tn(
                ACT[k, :, cols], dproj_b
            ).astype(BF16)
            dpre = dact * SL[k, :, cols]
            GV[k, 54 + q : 55 + q, :] = over_rows(dpre)
            dpre_b = dpre.astype(BF16)
            PG[k, cols, :] = dot_tn(normed, dpre_b).astype(BF16)

            @pl.when(core != k)
            def _():
                grad_copy(k, quarters + q).start()
                grad_copy(k, q).start()

            dn = dn + dot_nt(dpre_b, win[k, :, cols])

        @pl.when((core == 1) & (k == 0))
        def _():
            chip_sum(1)
            chip_vec_sum(1)

        xhat = XH[k]
        GV[k, 50:51, :] = over_rows(dn * xhat)
        GV[k, 51:52, :] = over_rows(dn)
        dxh = dn * row(k, 50)
        m1 = jnp.sum(dxh, axis=1, keepdims=True) * (1.0 / chans)
        m2 = jnp.sum(dxh * xhat, axis=1, keepdims=True) * (1.0 / chans)
        rstd = RSTD[k][:, 0:1]
        dconv = (dxh - m1 - xhat * m2) * rstd
        GV[k, 49:50, :] = over_rows(dconv)
        xpad[:, :, 8 : 8 + width, :] = dconv.reshape(pair, height, width, chans)
        for half in range(chans // 128):
            lanes = slice(half * 128, half * 128 + 128)
            acc = [G[k + 1, :, h, :, lanes].astype(F32) for h in range(height)]
            xs = [X[k, :, h, :, lanes].astype(F32) for h in range(height)]
            for j in range(7):
                shifted = [xpad[:, h, 11 - j : 11 - j + width, lanes] for h in range(height)]
                for i in range(7):
                    t = 7 * i + j
                    tap = vec[k, t, :, lanes][None]
                    total = None
                    for h in range(height):
                        if 0 <= h - i + 3 < height:
                            acc[h] = acc[h] + shifted[h - i + 3] * tap
                            term = xs[h] * shifted[h - i + 3]
                            total = term if total is None else total + term
                    GV[k, t : t + 1, lanes] = over_rows(total.reshape(pair * width, 128))
            for h in range(height):
                G[k, :, h, :, lanes] = acc[h].astype(BF16)

        @pl.when(core != k)
        def _():
            vec_copy(k).start()
            ig_copy(k).start()

        @pl.when(core == k)
        def _():
            IG[my_micros] = G[k]

        return carry

    lax.fori_loop(0, 2, backward, 0)

    @pl.when(sx == 1)
    def _():
        hop_g().start()

    @pl.when(core == 0)
    def _():
        chip_sum(0)
        chip_vec_sum(0)

    def z_copy(s):
        src = S.at[plane, pl.ds(s * zrows, zrows)]
        return copy(src, ZB.at[s], zsend.at[s], zrecv.at[s], {"z": z_at(offset(s))})

    for c, (lo, hi) in enumerate(chunks):

        @pl.loop(1, nplane)
        def _(r):
            plane_copy(c, r).wait_recv()

        for s in reversed(range(lo, hi)):
            at = slice(s * zrows, (s + 1) * zrows)
            acc = S[plane, at, :].astype(F32)
            for t in range(1, nplane):
                acc = acc + RB[t, at, :].astype(F32)
            if s > 0:
                S[plane, at, :] = acc.astype(BF16)
                z_copy(s).start()
            else:
                ZB[0] = acc.astype(BF16)

    def vec_up():
        r = lax.rem(owner - z + nz, nz)
        return copy(RBV.at[0], VZ.at[r], vsend, vrecv.at[r], {"z": owner})

    @pl.loop(1, nplane)
    def _(r):
        plane_vec_copy(r).wait_recv()

    vacc = SV[plane].astype(F32)
    for r in range(1, nplane):
        vacc = vacc + RBV[r].astype(F32)
    RBV[0] = vacc.astype(BF16)

    @pl.when(z != owner)
    def _():
        vec_up().start()

    def share_copy(s):
        return copy(
            GATH.at[plane, pl.ds(0, zrows)],
            GATH.at[plane, pl.ds(mirror(s, nz) * zrows, zrows)],
            asend.at[s], arecv.at[mirror(s, nz)], {"z": z_at(offset(s))},
        )

    def group_copy(g, r):
        lo, hi = groups[g]
        at = pl.ds(lo * zrows, (hi - lo) * zrows)
        return copy(
            GATH.at[plane, at], GATH.at[plane, at], gsend.at[g, r], grecv.at[g, r],
            plane_dev(r)[1],
        )

    for s in range(1, nz):
        z_copy(s).wait_recv()
    share = ZB[0].astype(F32)
    for s in range(1, nz):
        share = share + ZB[s].astype(F32)
    GATH[plane, 0:zrows, :] = share.astype(BF16)
    for s in reversed(range(1, nz)):
        share_copy(s).start()

    @pl.loop(1, nplane)
    def _(r):
        group_copy(0, r).start()

    SQS[2 * sx + core] = jnp.broadcast_to(jnp.sum(share * share), (1, 128))

    def vec_down(r):
        return copy(
            GATHV.at[plane], GATHV.at[plane], bsend.at[r], brecv, {"z": z_at(r)}
        )

    @pl.when(z == owner)
    def _():
        @pl.loop(1, nz)
        def _(r):
            copy(VZ.at[r], VZ.at[r], vsend, vrecv.at[r], {"z": owner}).wait_recv()

        total = RBV[0].astype(F32)
        for r in range(1, nz):
            total = total + VZ[r].astype(F32)
        GATHV[plane] = total.astype(BF16)

        @pl.loop(1, nz)
        def _(r):
            vec_down(r).start()

        SQS[2 * sx + core] = SQS[2 * sx + core] + jnp.broadcast_to(
            jnp.sum(total * total), (1, 128)
        )

    def sq_block(t):
        at = SQS.at[2 * sx + core]
        return copy(at, at, qsend.at[t], qrecv.at[t], (sib, far, diag)[t])

    def sq_z(r):
        at = SQZ.at[z]
        return copy(at, at, qzsend.at[r], qzrecv.at[r], {"z": z_at(r)})

    def sq_plane(r):
        at = SQP.at[plane]
        return copy(at, at, qpsend.at[r], qprecv.at[r], plane_dev(r)[1])

    for t in range(3):
        sq_block(t).start()

    def forward_group(g):
        lo, hi = groups[g]
        for s in range(lo, hi):
            at = GATH.at[plane, pl.ds(s * zrows, zrows)]
            copy(at, at, asend.at[s], arecv.at[s], sib).wait_recv()

        @pl.loop(1, nplane)
        def _(r):
            group_copy(g, r).start()

    forward_group(1)
    mates = (2 * sx + 1 - core, 2 * (1 - sx) + core, 2 * (1 - sx) + 1 - core)
    for t in range(3):
        at = SQS.at[mates[t]]
        copy(at, at, qsend.at[t], qrecv.at[t], sib).wait_recv()
    SQZ[z] = (SQS[0] + SQS[1]) + (SQS[2] + SQS[3])

    @pl.loop(1, nz)
    def _(r):
        sq_z(r).start()

    for g in range(2, len(groups)):
        forward_group(g)

    def vec_out(r):
        at = GATHV.at[plane]
        return copy(at, at, gvsend.at[r], gvrecv.at[r], plane_dev(r)[1])

    @pl.when(z != owner)
    def _():
        vec_down(1).wait_recv()

    @pl.loop(1, nplane)
    def _(r):
        vec_out(r).start()

    @pl.loop(1, nz)
    def _(r):
        at = SQZ.at[z_at(-r)]
        copy(at, at, qzsend.at[r], qzrecv.at[r], sib).wait_recv()

    total = SQZ[0]
    for t in range(1, nz):
        total = total + SQZ[t]
    SQP[plane] = total

    @pl.loop(1, nplane)
    def _(r):
        sq_plane(r).start()

    ig_copy(0).wait_recv()
    ig_ref[...] = IG[...]

    for c in wcopies:
        c.wait_send()
    hop_x().wait_send()
    ig_copy(0).wait_send()
    for t in range(2 * quarters):
        grad_copy(0, t).wait_send()
    vec_copy(0).wait_send()

    @pl.loop(1, nplane)
    def _(r):
        for c in range(len(chunks)):
            plane_copy(c, r).wait_send()
        plane_vec_copy(r).wait_send()

    for s in range(1, nz):
        z_copy(s).wait_send()
        share_copy(s).wait_send()

    @pl.when(z != owner)
    def _():
        vec_up().wait_send()

    @pl.when(z == owner)
    def _():
        @pl.loop(1, nz)
        def _(r):
            vec_down(r).wait_send()

    for t in range(3):
        sq_block(t).wait_send()

    @pl.loop(1, nz)
    def _(r):
        sq_z(r).wait_send()

    @pl.loop(1, nplane)
    def _(r):
        q = lax.rem(plane - r + nplane, nplane)
        for g, (lo, hi) in enumerate(groups):
            at = GATH.at[q, pl.ds(lo * zrows, (hi - lo) * zrows)]
            copy(at, at, gsend.at[g, r], grecv.at[g, r], sib).wait_recv()
        copy(GATHV.at[q], GATHV.at[q], gvsend.at[r], gvrecv.at[r], sib).wait_recv()
        copy(SQP.at[q], SQP.at[q], qpsend.at[r], qprecv.at[r], sib).wait_recv()

    gath_ref[...] = GATH[...]
    gathv_ref[...] = GATHV[...]
    total = SQP[0]
    for t in range(1, nplane):
        total = total + SQP[t]
    factor = jnp.minimum(1.0, (params**0.5) * lax.rsqrt(total + 1e-06))
    fac_ref[...] = jnp.broadcast_to(factor, fac_ref.shape)

    @pl.loop(1, nplane)
    def _(r):
        for g in range(len(groups)):
            group_copy(g, r).wait_send()
        vec_out(r).wait_send()
        sq_plane(r).wait_send()


def scale_kernel(nz, gath, gathv, fac, ig, o_in, o_out, o_vec, o_ig):
    nplane, part, chans = gath.shape
    hidden = o_in.shape[1]
    quarters = hidden // chans
    zrows = part // nz
    vlanes = gathv.shape[2]
    vcols = chans // vlanes
    z = lax.axis_index("z")
    f = fac[0:1, 0:1]
    per = chans // zrows
    for s in range(nz):
        q = lax.rem(z + offset(s) + nz, nz)
        for p in range(nplane):
            piece = gath[p, s * zrows : (s + 1) * zrows, :].astype(F32) * f
            first = p * part
            if first < hidden:
                if part <= chans:
                    at = pl.ds(pl.multiple_of(first % chans + q * zrows, zrows), zrows)
                    o_in[at, first // chans * chans : first // chans * chans + chans] = piece
                else:
                    for t in range(part // chans):
                        @pl.when(q // per == t)
                        def _():
                            at = pl.ds(pl.multiple_of(lax.rem(q, per) * zrows, zrows), zrows)
                            o_in[at, first + t * chans : first + t * chans + chans] = piece
            else:
                at = pl.ds(pl.multiple_of(first - hidden + q * zrows, zrows), zrows)
                o_out[at, :] = piece
    for p in range(nplane):
        at_row, at_col = (p // vcols) * VTILE, (p % vcols) * vlanes
        tile = gathv[p].astype(F32) * f
        for t in range(min(VTILE, o_vec.shape[0] - at_row)):
            o_vec[at_row + t, :, at_col : at_col + vlanes] = tile[t : t + 1, :]
    o_ig[...] = ig[...]


def per_device(dims, inputs, out_grad, w_in, w_out, vector_params):
    nz, ny, nx, params = dims
    nplane = ny * nx
    micros, _, height, width, chans = inputs.shape
    hidden = w_in.shape[2]
    vrows = vector_params.shape[1]
    pair = micros // 2
    rows = pair * height * width
    part = 2 * hidden // nplane
    zrows = part // nz
    vlanes = VPAD * chans // nplane // VTILE
    chunks, groups = spans(nz)
    maps = (micros, height, width, chans)
    small = (pair, height, width, chans)
    vm = pltpu.VMEM
    dma = pltpu.SemaphoreType.DMA
    in_vmem = pl.BlockSpec(memory_space=pltpu.VMEM)
    in_hbm = pl.BlockSpec(memory_space=pltpu.HBM)
    gath, gathv, fac, ig = pl.pallas_call(
        functools.partial(relay_kernel, dims),
        out_shape=(
            jax.ShapeDtypeStruct((nplane, part, chans), BF16),
            jax.ShapeDtypeStruct((nplane, VTILE, vlanes), BF16),
            jax.ShapeDtypeStruct((8, 128), F32),
            jax.ShapeDtypeStruct(maps, BF16),
        ),
        in_specs=[in_hbm] * 5,
        out_specs=(in_vmem,) * 4,
        scratch_shapes=[
            vm((2, chans, hidden), BF16),
            vm((2, hidden, chans), BF16),
            vm((2, vrows, 1, chans), F32),
            vm((3,) + small, BF16),
            vm((3,) + small, BF16),
            vm((pair, height, width + 16, chans), F32),
            vm(small, F32),
            vm((2, rows, chans), F32),
            vm((2, rows, 128), F32),
            vm((2, rows, chans), BF16),
            vm((2, rows, hidden), BF16),
            vm((2, rows, hidden), F32),
            vm((2, rows, chans), F32),
            vm((2, 2 * hidden, chans), BF16),
            vm((2, VPAD, chans), F32),
            vm((2 * hidden, chans), BF16),
            vm((VPAD, chans), F32),
            vm(maps, BF16),
            vm((nplane, part, chans), BF16),
            vm((nplane, part, chans), BF16),
            vm((nplane, VTILE, vlanes), BF16),
            vm((nplane, VTILE, vlanes), BF16),
            vm((nz, zrows, chans), BF16),
            vm((nz, VTILE, vlanes), BF16),
            vm((nplane, part, chans), BF16),
            vm((nplane, VTILE, vlanes), BF16),
            vm((4, 1, 128), F32),
            vm((nz, 1, 128), F32),
            vm((nplane, 1, 128), F32),
            dma((4,)),
            dma((3,)), dma((3,)),
            dma, dma,
            dma, dma,
            dma((2 * hidden // chans,)), dma((2 * hidden // chans,)),
            dma, dma,
            dma((len(chunks), nplane)), dma((len(chunks), nplane)),
            dma((nplane,)), dma((nplane,)),
            dma((nz,)), dma((nz,)),
            dma, dma((nz,)),
            dma((nz,)), dma,
            dma((nz,)), dma((nz,)),
            dma((len(groups), nplane)), dma((len(groups), nplane)),
            dma((nplane,)), dma((nplane,)),
            dma((3,)), dma((3,)),
            dma((nz,)), dma((nz,)),
            dma((nplane,)), dma((nplane,)),
        ],
        compiler_params=pltpu.CompilerParams(
            collective_id=0, has_side_effects=True, vmem_limit_bytes=60 * 1024 * 1024
        ),
        name="relay",
    )(
        inputs.reshape(maps), out_grad.reshape(maps), w_in[0], w_out[0],
        jnp.swapaxes(vector_params, 0, 1),
    )
    o_in, o_out, o_vec, o_ig = pl.pallas_call(
        functools.partial(scale_kernel, nz),
        out_shape=(
            jax.ShapeDtypeStruct((chans, hidden), F32),
            jax.ShapeDtypeStruct((hidden, chans), F32),
            jax.ShapeDtypeStruct((vrows, 1, chans), F32),
            jax.ShapeDtypeStruct(maps, BF16),
        ),
        in_specs=[in_vmem] * 4,
        out_specs=(in_vmem,) * 4,
        compiler_params=pltpu.CompilerParams(vmem_limit_bytes=60 * 1024 * 1024),
        name="scale",
    )(gath, gathv, fac, ig)
    return (
        o_ig.reshape((1, micros, 1, height, width, chans)),
        o_in[None],
        o_out[None],
        jnp.swapaxes(o_vec, 0, 1),
    )


def solution(mesh):
    nx = 2
    ny = 4
    nz = mesh.shape["dp"] // (nx * ny)
    return program_on(mesh, nz, ny, nx)


def program_on(mesh, nz, ny, nx, params=2156544):
    split = Mesh(mesh.devices.reshape(2, 2, nz, ny, nx), ("sx", "core", "z", "y", "xl"))
    dp = ("z", "y", "xl")
    seg = ("sx", "core")
    in_specs = (
        P(None, dp, None, None, None),
        P(None, dp, None, None, None),
        P(seg, None, None),
        P(seg, None, None),
        P(seg, None, None),
    )
    out_specs = (
        P(seg, None, dp, None, None, None),
        P(seg, None, None),
        P(seg, None, None),
        P(seg, None, None),
    )
    return jax.shard_map(
        functools.partial(per_device, (nz, ny, nx, params)),
        mesh=split, in_specs=in_specs, out_specs=out_specs, check_vma=False,
    )
```

time: 104 us -> 96.1 us (0.924); the launches traced: 104 us -> 94.7 us
  local copies, waits for them, and re-layouts: 5.41 us -> 0 us
  Pallas kernels: 97.7 us -> 94.1 us
    unnamed x10 -> x0, local copies, waits for them, and re-layouts: 5.41 us -> none
    pallas_call x1, Pallas kernels: 96.2 us -> 91.3 us  [per_device(): pl.pallas_call(functools.partial(relay_kernel, dims), out_shape=(jax.Shap...]
    pallas_call x1, Pallas kernels: 1.47 us -> 2.78 us  [per_device(): pl.pallas_call(functools.partial(scale_kernel, nz), out_shape=(jax.ShapeD...]
where the time goes in v1:
time: 96.1 us; the launch traced here: 94.7 us
  Pallas kernels  94.1 us (98%)
    pallas_call x1, Pallas kernels, per_device(): pl.pallas_call(functools.partial(relay_kernel, dims), out_shape=(jax.Shap...  91.3 us
    pallas_call x1, Pallas kernels, per_device(): pl.pallas_call(functools.partial(scale_kernel, nz), out_shape=(jax.ShapeD...  2.78 us

profile of v1, /device:TPU:6, one launch (start us, length us, event | category | flops | bytes accessed | tf_op | source)
XLA Modules:
  0.0 94.7 jit_solution(3090147595391599417)
XLA Ops:
  0.6 91.3 %relay.1 = (bf16[8,256,256]{2,1,0:T(8,128)(2,1)}, bf16[8,16,128]{2,1,0:T(8,128)(2,1)}, f32[8,128]{1,0:T(8,128)}, bf16[4,4,16,256]{3,2,1,0:T(8,128)(2,1)}) custom-call(bf16[4,4,16,256]{3,2,1,0:T(8,128)(2,1)} %bitcast.13, bf16[4,4,16,256]{3,2,1,0:T(8,128)(2,1)} %bitcast.14, bf16[256,1024]{1,0:T(8,128)(2,1)} %bitcast.11, bf16[1024,256]{1,0:T(8,128)(2,1)} %bitcast.12, ...), custom_call_target="tpu_custom_call" | custom-call | tf_op jit(solution)/shard_map/relay/pallas_call | solution.py:634
  92.0 2.8 %scale.1 = (f32[256,1024]{1,0:T(8,128)}, f32[1024,256]{1,0:T(8,128)}, f32[58,1,256]{2,1,0:T(1,128)}, bf16[4,4,16,256]{3,2,1,0:T(8,128)(2,1)}) custom-call(bf16[8,256,256]{2,1,0:T(8,128)(2,1)} %get-tuple-element.12.gath, bf16[8,16,128]{2,1,0:T(8,128)(2,1)} %get-tuple-element.13.gathv, f32[8,128]{1,0:T(8,128)} %get-tuple-element.14.fac, ...), custom_call_target="tpu_custom_call" | custom-call | tf_op jit(solution)/shard_map/scale/pallas_call | solution.py:700

commit v2 on v1

--- a/solution.py
+++ b/solution.py
@@ -52,7 +52,7 @@
     PG, GV, RG, RV, IG, S, RB, SV, RBV, ZB, VZ, GATH, GATHV, SQS, SQZ, SQP,
     load_sem, wsend, wrecv, hsend, hrecv, isend, irecv, csend, crecv, cvsend, cvrecv,
     psend, precv, pvsend, pvrecv, zsend, zrecv, vsend, vrecv, bsend, brecv, asend, arecv,
-    gsend, grecv, gvsend, gvrecv, qsend, qrecv, qzsend, qzrecv, qpsend, qprecv,
+    gsend, grecv, gvsend, gvrecv, qsend, qrecv, qzsend, qzrecv, qpsend, qprecv, store_sem,
 ):
     nz, ny, nx, params = dims
     nplane = ny * nx
@@ -301,7 +301,7 @@
 
             dn = dn + dot_nt(dpre_b, win[k, :, cols])
 
-        @pl.when((core == 1) & (k == 0))
+        @pl.when((sx == 0) & (core == 1) & (k == 0))
         def _():
             chip_sum(1)
             chip_vec_sum(1)
@@ -351,11 +351,12 @@
     @pl.when(sx == 1)
     def _():
         hop_g().start()
-
-    @pl.when(core == 0)
-    def _():
-        chip_sum(0)
-        chip_vec_sum(0)
+        hop_g().wait_send()
+
+    @pl.when((core == 0) | (sx == 1))
+    def _():
+        chip_sum(core)
+        chip_vec_sum(core)
 
     def z_copy(s):
         src = S.at[plane, pl.ds(s * zrows, zrows)]
@@ -514,12 +515,21 @@
     def _(r):
         sq_plane(r).start()
 
+    def store(q):
+        return pltpu.make_async_copy(GATH.at[q], gath_ref.at[q], store_sem.at[q])
+
+    store(plane).start()
     ig_copy(0).wait_recv()
-    ig_ref[...] = IG[...]
+    ig_out = pltpu.make_async_copy(IG, ig_ref, load_sem.at[4])
+    ig_out.start()
 
     for c in wcopies:
         c.wait_send()
-    hop_x().wait_send()
+
+    @pl.when(sx == 0)
+    def _():
+        hop_x().wait_send()
+
     ig_copy(0).wait_send()
     for t in range(2 * quarters):
         grad_copy(0, t).wait_send()
@@ -558,10 +568,10 @@
         for g, (lo, hi) in enumerate(groups):
             at = GATH.at[q, pl.ds(lo * zrows, (hi - lo) * zrows)]
             copy(at, at, gsend.at[g, r], grecv.at[g, r], sib).wait_recv()
+        store(q).start()
         copy(GATHV.at[q], GATHV.at[q], gvsend.at[r], gvrecv.at[r], sib).wait_recv()
         copy(SQP.at[q], SQP.at[q], qpsend.at[r], qprecv.at[r], sib).wait_recv()
 
-    gath_ref[...] = GATH[...]
     gathv_ref[...] = GATHV[...]
     total = SQP[0]
     for t in range(1, nplane):
@@ -576,40 +586,34 @@
         vec_out(r).wait_send()
         sq_plane(r).wait_send()
 
+    @pl.loop(0, nplane)
+    def _(q):
+        store(q).wait()
+
+    ig_out.wait()
+
 
 def scale_kernel(nz, gath, gathv, fac, ig, o_in, o_out, o_vec, o_ig):
-    nplane, part, chans = gath.shape
-    hidden = o_in.shape[1]
-    quarters = hidden // chans
-    zrows = part // nz
-    vlanes = gathv.shape[2]
+    nplane, _, vlanes = gathv.shape
+    chans = gath.shape[3]
+    zrows = gath.shape[2] // nz
     vcols = chans // vlanes
     z = lax.axis_index("z")
     f = fac[0:1, 0:1]
-    per = chans // zrows
     for s in range(nz):
         q = lax.rem(z + offset(s) + nz, nz)
+        at = pl.ds(pl.multiple_of(q * zrows, zrows), zrows)
+        o_in[at, :] = gath[0, 0, s * zrows : (s + 1) * zrows, :].astype(F32) * f
+        o_out[at, :] = gath[1, 0, s * zrows : (s + 1) * zrows, :].astype(F32) * f
+
+    @pl.when(pl.program_id(0) == 0)
+    def _():
         for p in range(nplane):
-            piece = gath[p, s * zrows : (s + 1) * zrows, :].astype(F32) * f
-            first = p * part
-            if first < hidden:
-                if part <= chans:
-                    at = pl.ds(pl.multiple_of(first % chans + q * zrows, zrows), zrows)
-                    o_in[at, first // chans * chans : first // chans * chans + chans] = piece
-                else:
-                    for t in range(part // chans):
-                        @pl.when(q // per == t)
-                        def _():
-                            at = pl.ds(pl.multiple_of(lax.rem(q, per) * zrows, zrows), zrows)
-                            o_in[at, first + t * chans : first + t * chans + chans] = piece
-            else:
-                at = pl.ds(pl.multiple_of(first - hidden + q * zrows, zrows), zrows)
-                o_out[at, :] = piece
-    for p in range(nplane):
-        at_row, at_col = (p // vcols) * VTILE, (p % vcols) * vlanes
-        tile = gathv[p].astype(F32) * f
-        for t in range(min(VTILE, o_vec.shape[0] - at_row)):
-            o_vec[at_row + t, :, at_col : at_col + vlanes] = tile[t : t + 1, :]
+            at_row, at_col = (p // vcols) * VTILE, (p % vcols) * vlanes
+            tile = gathv[p].astype(F32) * f
+            for t in range(min(VTILE, o_vec.shape[0] - at_row)):
+                o_vec[at_row + t, :, at_col : at_col + vlanes] = tile[t : t + 1, :]
+
     o_ig[...] = ig[...]
 
 
@@ -640,7 +644,7 @@
             jax.ShapeDtypeStruct(maps, BF16),
         ),
         in_specs=[in_hbm] * 5,
-        out_specs=(in_vmem,) * 4,
+        out_specs=(in_hbm, in_vmem, in_vmem, in_hbm),
         scratch_shapes=[
             vm((2, chans, hidden), BF16),
             vm((2, hidden, chans), BF16),
@@ -671,7 +675,7 @@
             vm((4, 1, 128), F32),
             vm((nz, 1, 128), F32),
             vm((nplane, 1, 128), F32),
-            dma((4,)),
+            dma((5,)),
             dma((3,)), dma((3,)),
             dma, dma,
             dma, dma,
@@ -688,6 +692,7 @@
             dma((3,)), dma((3,)),
             dma((nz,)), dma((nz,)),
             dma((nplane,)), dma((nplane,)),
+            dma((nplane,)),
         ],
         compiler_params=pltpu.CompilerParams(
             collective_id=0, has_side_effects=True, vmem_limit_bytes=60 * 1024 * 1024
@@ -697,6 +702,7 @@
         inputs.reshape(maps), out_grad.reshape(maps), w_in[0], w_out[0],
         jnp.swapaxes(vector_params, 0, 1),
     )
+    quarters = hidden // chans
     o_in, o_out, o_vec, o_ig = pl.pallas_call(
         functools.partial(scale_kernel, nz),
         out_shape=(
@@ -705,11 +711,22 @@
             jax.ShapeDtypeStruct((vrows, 1, chans), F32),
             jax.ShapeDtypeStruct(maps, BF16),
         ),
-        in_specs=[in_vmem] * 4,
-        out_specs=(in_vmem,) * 4,
+        grid=(quarters,),
+        in_specs=[
+            pl.BlockSpec((2, 1, chans, chans), lambda t: (0, t, 0, 0)),
+            pl.BlockSpec((nplane, VTILE, vlanes), lambda t: (0, 0, 0)),
+            pl.BlockSpec((8, 128), lambda t: (0, 0)),
+            pl.BlockSpec((1,) + maps[1:], lambda t: (t, 0, 0, 0)),
+        ],
+        out_specs=(
+            pl.BlockSpec((chans, chans), lambda t: (0, t)),
+            pl.BlockSpec((chans, chans), lambda t: (t, 0)),
+            pl.BlockSpec((vrows, 1, chans), lambda t: (0, 0, 0)),
+            pl.BlockSpec((1,) + maps[1:], lambda t: (t, 0, 0, 0)),
+        ),
         compiler_params=pltpu.CompilerParams(vmem_limit_bytes=60 * 1024 * 1024),
         name="scale",
-    )(gath, gathv, fac, ig)
+    )(gath.reshape(2, quarters, chans, chans), gathv, fac, ig)
     return (
         o_ig.reshape((1, micros, 1, height, width, chans)),
         o_in[None],

time: 96.1 us -> 85.3 us (0.89); the launches traced: 94.7 us -> 85 us
  Pallas kernels: 94.1 us -> 84.4 us
    pallas_call x1, Pallas kernels: 91.3 us -> 80.6 us  [per_device(): pl.pallas_call(functools.partial(relay_kernel, dims), out_shape=(jax.Shap...]
where the time goes in v2:
time: 85.3 us; the launch traced here: 85 us
  Pallas kernels  84.4 us (99%)
    pallas_call x1, Pallas kernels, per_device(): pl.pallas_call(functools.partial(relay_kernel, dims), out_shape=(jax.Shap...  80.6 us
    pallas_call x1, Pallas kernels, per_device(): pl.pallas_call(functools.partial(scale_kernel, nz), out_shape=(jax.ShapeD...  3.74 us

profile of v2, /device:TPU:6, one launch (start us, length us, event | category | flops | bytes accessed | tf_op | source)
XLA Modules:
  0.0 85.0 jit_solution(3108685263460086550)
XLA Ops:
  0.6 80.6 %relay.1 = (bf16[8,256,256]{2,1,0:T(8,128)(2,1)}, bf16[8,16,128]{2,1,0:T(8,128)(2,1)}, f32[8,128]{1,0:T(8,128)}, bf16[4,4,16,256]{3,2,1,0:T(8,128)(2,1)}) custom-call(bf16[4,4,16,256]{3,2,1,0:T(8,128)(2,1)} %bitcast.15, bf16[4,4,16,256]{3,2,1,0:T(8,128)(2,1)} %bitcast.16, bf16[256,1024]{1,0:T(8,128)(2,1)} %bitcast.13, bf16[1024,256]{1,0:T(8,128)(2,1)} %bitcast.14, ...), custom_call_target="tpu_custom_call" | custom-call | tf_op jit(solution)/shard_map/relay/pallas_call | solution.py:638
  81.3 3.7 %scale.1 = (f32[256,1024]{1,0:T(8,128)}, f32[1024,256]{1,0:T(8,128)}, f32[58,1,256]{2,1,0:T(1,128)}, bf16[4,4,16,256]{3,2,1,0:T(8,128)(2,1)}) custom-call(bf16[2,4,256,256]{3,2,1,0:T(8,128)(2,1)} %bitcast.12, bf16[8,16,128]{2,1,0:T(8,128)(2,1)} %get-tuple-element.13.gathv, f32[8,128]{1,0:T(8,128)} %get-tuple-element.14.fac, ...), custom_call_target="tpu_custom_call" | custom-call | tf_op jit(solution)/shard_map/scale/pallas_call | solution.py:706

commit v3 on v1

--- a/solution.py
+++ b/solution.py
@@ -52,7 +52,7 @@
     PG, GV, RG, RV, IG, S, RB, SV, RBV, ZB, VZ, GATH, GATHV, SQS, SQZ, SQP,
     load_sem, wsend, wrecv, hsend, hrecv, isend, irecv, csend, crecv, cvsend, cvrecv,
     psend, precv, pvsend, pvrecv, zsend, zrecv, vsend, vrecv, bsend, brecv, asend, arecv,
-    gsend, grecv, gvsend, gvrecv, qsend, qrecv, qzsend, qzrecv, qpsend, qprecv,
+    gsend, grecv, gvsend, gvrecv, qsend, qrecv, qzsend, qzrecv, qpsend, qprecv, store_sem, known_sem,
 ):
     nz, ny, nx, params = dims
     nplane = ny * nx
@@ -118,9 +118,8 @@
     def hello(dev):
         pl.semaphore_signal(barrier, inc=1, device_id=dev, device_id_type=pl.DeviceIdType.MESH)
 
-    @pl.loop(1, nz)
-    def _(r):
-        hello({"z": z_at(r)})
+    hello({"z": z_at(1)})
+    hello({"z": z_at(-1)})
 
     @pl.loop(1, nplane)
     def _(r):
@@ -143,7 +142,7 @@
     def _():
         load_g().wait()
 
-    pl.semaphore_wait(barrier, 3 + (nplane - 1) + (nz - 1))
+    pl.semaphore_wait(barrier, 3 + (nplane - 1) + 2)
 
     wcopies = [
         copy(vec_ref, vec.at[core], wsend.at[0], wrecv.at[0], sib),
@@ -152,6 +151,21 @@
     ]
     for c in wcopies:
         c.start()
+
+    reaches = [1 << t for t in range(8) if (1 << t) < nz // 2]
+
+    def tell(t):
+        for by in (reaches[t], -reaches[t]):
+            pl.semaphore_signal(
+                known_sem.at[t], inc=1, device_id={"z": z_at(by)},
+                device_id_type=pl.DeviceIdType.MESH,
+            )
+
+    def heard(t):
+        pl.semaphore_wait(known_sem.at[t], 2)
+
+    if reaches:
+        tell(0)
 
     def hop_x():
         return copy(X.at[2], X.at[0], hsend, hrecv, far)
@@ -218,6 +232,9 @@
         return carry
 
     lax.fori_loop(0, 2, forward, 0)
+    if len(reaches) > 1:
+        heard(0)
+        tell(1)
 
     @pl.when(sx == 0)
     def _():
@@ -276,6 +293,18 @@
 
     def backward(step, carry):
         k = 1 - step
+
+        if len(reaches) > 2:
+
+            @pl.when(step == 1)
+            def _():
+                heard(1)
+                tell(2)
+
+        @pl.when((sx == 0) & (core == 1) & (k == 0))
+        def _():
+            chip_sum(1)
+
         gf = G[k + 1].astype(F32).reshape(rows, chans)
         GV[k, 53:54, :] = over_rows(gf * PJ[k])
         dproj = gf * row(k, 53)
@@ -301,9 +330,8 @@
 
             dn = dn + dot_nt(dpre_b, win[k, :, cols])
 
-        @pl.when((core == 1) & (k == 0))
+        @pl.when((sx == 0) & (core == 1) & (k == 0))
         def _():
-            chip_sum(1)
             chip_vec_sum(1)
 
         xhat = XH[k]
@@ -351,15 +379,19 @@
     @pl.when(sx == 1)
     def _():
         hop_g().start()
-
-    @pl.when(core == 0)
-    def _():
-        chip_sum(0)
-        chip_vec_sum(0)
+        hop_g().wait_send()
+
+    @pl.when((core == 0) | (sx == 1))
+    def _():
+        chip_sum(core)
+        chip_vec_sum(core)
 
     def z_copy(s):
         src = S.at[plane, pl.ds(s * zrows, zrows)]
         return copy(src, ZB.at[s], zsend.at[s], zrecv.at[s], {"z": z_at(offset(s))})
+
+    if reaches:
+        heard(len(reaches) - 1)
 
     for c, (lo, hi) in enumerate(chunks):
 
@@ -514,12 +546,21 @@
     def _(r):
         sq_plane(r).start()
 
+    def store(q):
+        return pltpu.make_async_copy(GATH.at[q], gath_ref.at[q], store_sem.at[q])
+
+    store(plane).start()
     ig_copy(0).wait_recv()
-    ig_ref[...] = IG[...]
+    ig_out = pltpu.make_async_copy(IG, ig_ref, load_sem.at[4])
+    ig_out.start()
 
     for c in wcopies:
         c.wait_send()
-    hop_x().wait_send()
+
+    @pl.when(sx == 0)
+    def _():
+        hop_x().wait_send()
+
     ig_copy(0).wait_send()
     for t in range(2 * quarters):
         grad_copy(0, t).wait_send()
@@ -558,10 +599,10 @@
         for g, (lo, hi) in enumerate(groups):
             at = GATH.at[q, pl.ds(lo * zrows, (hi - lo) * zrows)]
             copy(at, at, gsend.at[g, r], grecv.at[g, r], sib).wait_recv()
+        store(q).start()
         copy(GATHV.at[q], GATHV.at[q], gvsend.at[r], gvrecv.at[r], sib).wait_recv()
         copy(SQP.at[q], SQP.at[q], qpsend.at[r], qprecv.at[r], sib).wait_recv()
 
-    gath_ref[...] = GATH[...]
     gathv_ref[...] = GATHV[...]
     total = SQP[0]
     for t in range(1, nplane):
@@ -575,6 +616,12 @@
             group_copy(g, r).wait_send()
         vec_out(r).wait_send()
         sq_plane(r).wait_send()
+
+    @pl.loop(0, nplane)
+    def _(q):
+        store(q).wait()
+
+    ig_out.wait()
 
 
 def scale_kernel(nz, gath, gathv, fac, ig, o_in, o_out, o_vec, o_ig):
@@ -640,7 +687,7 @@
             jax.ShapeDtypeStruct(maps, BF16),
         ),
         in_specs=[in_hbm] * 5,
-        out_specs=(in_vmem,) * 4,
+        out_specs=(in_hbm, in_vmem, in_vmem, in_hbm),
         scratch_shapes=[
             vm((2, chans, hidden), BF16),
             vm((2, hidden, chans), BF16),
@@ -671,7 +718,7 @@
             vm((4, 1, 128), F32),
             vm((nz, 1, 128), F32),
             vm((nplane, 1, 128), F32),
-            dma((4,)),
+            dma((5,)),
             dma((3,)), dma((3,)),
             dma, dma,
             dma, dma,
@@ -688,6 +735,8 @@
             dma((3,)), dma((3,)),
             dma((nz,)), dma((nz,)),
             dma((nplane,)), dma((nplane,)),
+            dma((nplane,)),
+            pltpu.SemaphoreType.REGULAR((3,)),
         ],
         compiler_params=pltpu.CompilerParams(
             collective_id=0, has_side_effects=True, vmem_limit_bytes=60 * 1024 * 1024

time: 96.1 us -> 81.6 us (0.85); the launches traced: 94.7 us -> 81.2 us
  Pallas kernels: 94.1 us -> 80.6 us
    pallas_call x1, Pallas kernels: 91.3 us -> 77.8 us  [per_device(): pl.pallas_call(functools.partial(relay_kernel, dims), out_shape=(jax.Shap...]
where the time goes in v3:
time: 81.6 us; the launch traced here: 81.2 us
  Pallas kernels  80.6 us (99%)
    pallas_call x1, Pallas kernels, per_device(): pl.pallas_call(functools.partial(relay_kernel, dims), out_shape=(jax.Shap...  77.8 us
    pallas_call x1, Pallas kernels, per_device(): pl.pallas_call(functools.partial(scale_kernel, nz), out_shape=(jax.ShapeD...  2.78 us

profile of v3, /device:TPU:6, one launch (start us, length us, event | category | flops | bytes accessed | tf_op | source)
XLA Modules:
  0.0 81.2 jit_solution(8340881585328953943)
XLA Ops:
  0.6 77.8 %relay.1 = (bf16[8,256,256]{2,1,0:T(8,128)(2,1)}, bf16[8,16,128]{2,1,0:T(8,128)(2,1)}, f32[8,128]{1,0:T(8,128)}, bf16[4,4,16,256]{3,2,1,0:T(8,128)(2,1)}) custom-call(bf16[4,4,16,256]{3,2,1,0:T(8,128)(2,1)} %bitcast.13, bf16[4,4,16,256]{3,2,1,0:T(8,128)(2,1)} %bitcast.14, bf16[256,1024]{1,0:T(8,128)(2,1)} %bitcast.11, bf16[1024,256]{1,0:T(8,128)(2,1)} %bitcast.12, ...), custom_call_target="tpu_custom_call" | custom-call | tf_op jit(solution)/shard_map/relay/pallas_call | solution.py:681
  78.4 2.8 %scale.1 = (f32[256,1024]{1,0:T(8,128)}, f32[1024,256]{1,0:T(8,128)}, f32[58,1,256]{2,1,0:T(1,128)}, bf16[4,4,16,256]{3,2,1,0:T(8,128)(2,1)}) custom-call(bf16[8,256,256]{2,1,0:T(8,128)(2,1)} %get-tuple-element.12.gath, bf16[8,16,128]{2,1,0:T(8,128)(2,1)} %get-tuple-element.13.gathv, f32[8,128]{1,0:T(8,128)} %get-tuple-element.14.fac, ...), custom_call_target="tpu_custom_call" | custom-call | tf_op jit(solution)/shard_map/scale/pallas_call | solution.py:749

commit v4 on v3

--- a/solution.py
+++ b/solution.py
@@ -32,7 +32,7 @@
 
 def spans(nz):
     if nz == 16:
-        return ((11, 16), (6, 11), (0, 6)), ((0, 1), (1, 5), (5, 9), (9, 13), (13, 16))
+        return ((13, 16), (10, 13), (7, 10), (4, 7), (0, 4)), ((0, 1), (1, 5), (5, 9), (9, 13), (13, 16))
     return ((1, nz), (0, 1)), ((0, 1), (1, nz))
 
 
@@ -130,8 +130,9 @@
     hello(sib)
 
     zero_side = jnp.zeros((pair, height, 8, chans), F32)
-    xpad[:, :, 0:8, :] = zero_side
-    xpad[:, :, 8 + width : 16 + width, :] = zero_side
+    for k in range(2):
+        xpad[k, :, :, 0:8, :] = zero_side
+        xpad[k, :, :, 8 + width : 16 + width, :] = zero_side
     GV[...] = jnp.zeros(GV.shape, F32)
 
     @pl.when(sx == 0)
@@ -181,22 +182,22 @@
         return vec[k, t]
 
     def forward(k, carry):
-        @pl.when(core == k)
-        def _():
-            for c in loads:
-                c.wait()
-
-        @pl.when(core != k)
-        def _():
-            for c in wcopies:
-                c.wait_recv()
-
-        xpad[:, :, 8 : 8 + width, :] = X[k].astype(F32)
+        def ready(t):
+            @pl.when(core == k)
+            def _():
+                loads[t].wait()
+
+            @pl.when(core != k)
+            def _():
+                wcopies[t].wait_recv()
+
+        xpad[k, :, :, 8 : 8 + width, :] = X[k].astype(F32)
+        ready(0)
         for half in range(chans // 128):
             lanes = slice(half * 128, half * 128 + 128)
             acc = [None] * height
             for j in range(7):
-                shifted = [xpad[:, h, 5 + j : 5 + j + width, lanes] for h in range(height)]
+                shifted = [xpad[k, :, h, 5 + j : 5 + j + width, lanes] for h in range(height)]
                 for i in range(7):
                     tap = vec[k, 7 * i + j, :, lanes][None]
                     for h in range(height):
@@ -216,6 +217,8 @@
         RSTD[k] = jnp.broadcast_to(rstd, (rows, 128))
         normed = (xhat * row(k, 50) + row(k, 51)).astype(BF16)
         NB[k] = normed
+        ready(1)
+        ready(2)
         proj = jnp.zeros((rows, chans), F32)
         for q in range(quarters):
             cols = slice(q * chans, (q + 1) * chans)
@@ -330,10 +333,6 @@
 
             dn = dn + dot_nt(dpre_b, win[k, :, cols])
 
-        @pl.when((sx == 0) & (core == 1) & (k == 0))
-        def _():
-            chip_vec_sum(1)
-
         xhat = XH[k]
         GV[k, 50:51, :] = over_rows(dn * xhat)
         GV[k, 51:52, :] = over_rows(dn)
@@ -343,34 +342,49 @@
         rstd = RSTD[k][:, 0:1]
         dconv = (dxh - m1 - xhat * m2) * rstd
         GV[k, 49:50, :] = over_rows(dconv)
-        xpad[:, :, 8 : 8 + width, :] = dconv.reshape(pair, height, width, chans)
+        xpad[k, :, :, 8 : 8 + width, :] = dconv.reshape(pair, height, width, chans)
         for half in range(chans // 128):
             lanes = slice(half * 128, half * 128 + 128)
             acc = [G[k + 1, :, h, :, lanes].astype(F32) for h in range(height)]
+            for j in range(7):
+                shifted = [xpad[k, :, h, 11 - j : 11 - j + width, lanes] for h in range(height)]
+                for i in range(7):
+                    tap = vec[k, 7 * i + j, :, lanes][None]
+                    for h in range(height):
+                        if 0 <= h - i + 3 < height:
+                            acc[h] = acc[h] + shifted[h - i + 3] * tap
+            for h in range(height):
+                G[k, :, h, :, lanes] = acc[h].astype(BF16)
+
+        @pl.when(core != k)
+        def _():
+            ig_copy(k).start()
+
+        @pl.when(core == k)
+        def _():
+            IG[my_micros] = G[k]
+
+        return carry
+
+    def tap_grads(step, carry):
+        k = 1 - step
+        for half in range(chans // 128):
+            lanes = slice(half * 128, half * 128 + 128)
             xs = [X[k, :, h, :, lanes].astype(F32) for h in range(height)]
             for j in range(7):
-                shifted = [xpad[:, h, 11 - j : 11 - j + width, lanes] for h in range(height)]
+                shifted = [xpad[k, :, h, 11 - j : 11 - j + width, lanes] for h in range(height)]
                 for i in range(7):
                     t = 7 * i + j
-                    tap = vec[k, t, :, lanes][None]
                     total = None
                     for h in range(height):
                         if 0 <= h - i + 3 < height:
-                            acc[h] = acc[h] + shifted[h - i + 3] * tap
                             term = xs[h] * shifted[h - i + 3]
                             total = term if total is None else total + term
                     GV[k, t : t + 1, lanes] = over_rows(total.reshape(pair * width, 128))
-            for h in range(height):
-                G[k, :, h, :, lanes] = acc[h].astype(BF16)
 
         @pl.when(core != k)
         def _():
             vec_copy(k).start()
-            ig_copy(k).start()
-
-        @pl.when(core == k)
-        def _():
-            IG[my_micros] = G[k]
 
         return carry
 
@@ -379,12 +393,18 @@
     @pl.when(sx == 1)
     def _():
         hop_g().start()
+
+    lax.fori_loop(0, 2, tap_grads, 0)
+
+    @pl.when(sx == 1)
+    def _():
         hop_g().wait_send()
 
     @pl.when((core == 0) | (sx == 1))
     def _():
         chip_sum(core)
-        chip_vec_sum(core)
+
+    chip_vec_sum(core)
 
     def z_copy(s):
         src = S.at[plane, pl.ds(s * zrows, zrows)]
@@ -448,7 +468,7 @@
     for s in range(1, nz):
         share = share + ZB[s].astype(F32)
     GATH[plane, 0:zrows, :] = share.astype(BF16)
-    for s in reversed(range(1, nz)):
+    for s in [*range(1, min(5, nz)), *reversed(range(5, nz))]:
         share_copy(s).start()
 
     @pl.loop(1, nplane)
@@ -694,7 +714,7 @@
             vm((2, vrows, 1, chans), F32),
             vm((3,) + small, BF16),
             vm((3,) + small, BF16),
-            vm((pair, height, width + 16, chans), F32),
+            vm((2, pair, height, width + 16, chans), F32),
             vm(small, F32),
             vm((2, rows, chans), F32),
             vm((2, rows, 128), F32),

time: 81.6 us -> 80.3 us (0.984)
  Pallas kernels: 80.6 us -> 79.5 us
    pallas_call x1, Pallas kernels: 77.8 us -> 76.7 us  [per_device(): pl.pallas_call(functools.partial(relay_kernel, dims), out_shape=(jax.Shap...]
where the time goes in v4:
time: 80.3 us; the launch traced here: 80.1 us
  Pallas kernels  79.5 us (99%)
    pallas_call x1, Pallas kernels, per_device(): pl.pallas_call(functools.partial(relay_kernel, dims), out_shape=(jax.Shap...  76.7 us
    pallas_call x1, Pallas kernels, per_device(): pl.pallas_call(functools.partial(scale_kernel, nz), out_shape=(jax.ShapeD...  2.78 us

profile of v4, /device:TPU:6, one launch (start us, length us, event | category | flops | bytes accessed | tf_op | source)
XLA Modules:
  0.0 80.1 jit_solution(15419760531503198272)
XLA Ops:
  0.6 76.7 %relay.1 = (bf16[8,256,256]{2,1,0:T(8,128)(2,1)}, bf16[8,16,128]{2,1,0:T(8,128)(2,1)}, f32[8,128]{1,0:T(8,128)}, bf16[4,4,16,256]{3,2,1,0:T(8,128)(2,1)}) custom-call(bf16[4,4,16,256]{3,2,1,0:T(8,128)(2,1)} %bitcast.13, bf16[4,4,16,256]{3,2,1,0:T(8,128)(2,1)} %bitcast.14, bf16[256,1024]{1,0:T(8,128)(2,1)} %bitcast.11, bf16[1024,256]{1,0:T(8,128)(2,1)} %bitcast.12, ...), custom_call_target="tpu_custom_call" | custom-call | tf_op jit(solution)/shard_map/relay/pallas_call | solution.py:701
  77.3 2.8 %scale.1 = (f32[256,1024]{1,0:T(8,128)}, f32[1024,256]{1,0:T(8,128)}, f32[58,1,256]{2,1,0:T(1,128)}, bf16[4,4,16,256]{3,2,1,0:T(8,128)(2,1)}) custom-call(bf16[8,256,256]{2,1,0:T(8,128)(2,1)} %get-tuple-element.12.gath, bf16[8,16,128]{2,1,0:T(8,128)(2,1)} %get-tuple-element.13.gathv, f32[8,128]{1,0:T(8,128)} %get-tuple-element.14.fac, ...), custom_call_target="tpu_custom_call" | custom-call | tf_op jit(solution)/shard_map/scale/pallas_call | solution.py:769

commit v5 on v4

--- a/solution.py
+++ b/solution.py
@@ -264,10 +264,15 @@
         q, dev = plane_dev(r)
         return copy(SV.at[q], RBV.at[r], pvsend.at[r], pvrecv.at[r], dev)
 
-    def chip_sum(k):
-        for t in range(2 * quarters):
-            grad_copy(k, t).wait_recv()
-        for c, (lo, hi) in enumerate(chunks):
+    every = range(len(chunks))
+    early, late = every[:2], every[2:]
+
+    def chip_sum(k, some):
+        if 0 in some:
+            for t in range(2 * quarters):
+                grad_copy(k, t).wait_recv()
+        for c in some:
+            lo, hi = chunks[c]
 
             @pl.loop(1, nplane + 1)
             def _(r):
@@ -306,7 +311,7 @@
 
         @pl.when((sx == 0) & (core == 1) & (k == 0))
         def _():
-            chip_sum(1)
+            chip_sum(1, every)
 
         gf = G[k + 1].astype(F32).reshape(rows, chans)
         GV[k, 53:54, :] = over_rows(gf * PJ[k])
@@ -402,9 +407,13 @@
 
     @pl.when((core == 0) | (sx == 1))
     def _():
-        chip_sum(core)
+        chip_sum(core, early)
 
     chip_vec_sum(core)
+
+    @pl.when((core == 0) | (sx == 1))
+    def _():
+        chip_sum(core, late)
 
     def z_copy(s):
         src = S.at[plane, pl.ds(s * zrows, zrows)]
@@ -413,7 +422,27 @@
     if reaches:
         heard(len(reaches) - 1)
 
+    def vec_up():
+        r = lax.rem(owner - z + nz, nz)
+        return copy(RBV.at[0], VZ.at[r], vsend, vrecv.at[r], {"z": owner})
+
+    def vec_share():
+        @pl.loop(1, nplane)
+        def _(r):
+            plane_vec_copy(r).wait_recv()
+
+        vacc = SV[plane].astype(F32)
+        for r in range(1, nplane):
+            vacc = vacc + RBV[r].astype(F32)
+        RBV[0] = vacc.astype(BF16)
+
+        @pl.when(z != owner)
+        def _():
+            vec_up().start()
+
     for c, (lo, hi) in enumerate(chunks):
+        if c == min(2, len(chunks) - 1):
+            vec_share()
 
         @pl.loop(1, nplane)
         def _(r):
@@ -429,23 +458,6 @@
                 z_copy(s).start()
             else:
                 ZB[0] = acc.astype(BF16)
-
-    def vec_up():
-        r = lax.rem(owner - z + nz, nz)
-        return copy(RBV.at[0], VZ.at[r], vsend, vrecv.at[r], {"z": owner})
-
-    @pl.loop(1, nplane)
-    def _(r):
-        plane_vec_copy(r).wait_recv()
-
-    vacc = SV[plane].astype(F32)
-    for r in range(1, nplane):
-        vacc = vacc + RBV[r].astype(F32)
-    RBV[0] = vacc.astype(BF16)
-
-    @pl.when(z != owner)
-    def _():
-        vec_up().start()
 
     def share_copy(s):
         return copy(

time: 80.3 us -> 78 us (0.971)
  Pallas kernels: 79.5 us -> 76.5 us
    pallas_call x1, Pallas kernels: 76.7 us -> 73.8 us  [per_device(): pl.pallas_call(functools.partial(relay_kernel, dims), out_shape=(jax.Shap...]
where the time goes in v5:
time: 78 us; the launch traced here: 77.2 us
  Pallas kernels  76.5 us (98%)
    pallas_call x1, Pallas kernels, per_device(): pl.pallas_call(functools.partial(relay_kernel, dims), out_shape=(jax.Shap...  73.8 us
    pallas_call x1, Pallas kernels, per_device(): pl.pallas_call(functools.partial(scale_kernel, nz), out_shape=(jax.ShapeD...  2.78 us

profile of v5, /device:TPU:6, one launch (start us, length us, event | category | flops | bytes accessed | tf_op | source)
XLA Modules:
  0.0 77.2 jit_solution(17593061223641379035)
XLA Ops:
  0.6 73.8 %relay.1 = (bf16[8,256,256]{2,1,0:T(8,128)(2,1)}, bf16[8,16,128]{2,1,0:T(8,128)(2,1)}, f32[8,128]{1,0:T(8,128)}, bf16[4,4,16,256]{3,2,1,0:T(8,128)(2,1)}) custom-call(bf16[4,4,16,256]{3,2,1,0:T(8,128)(2,1)} %bitcast.13, bf16[4,4,16,256]{3,2,1,0:T(8,128)(2,1)} %bitcast.14, bf16[256,1024]{1,0:T(8,128)(2,1)} %bitcast.11, bf16[1024,256]{1,0:T(8,128)(2,1)} %bitcast.12, ...), custom_call_target="tpu_custom_call" | custom-call | tf_op jit(solution)/shard_map/relay/pallas_call | solution.py:713
  74.4 2.8 %scale.1 = (f32[256,1024]{1,0:T(8,128)}, f32[1024,256]{1,0:T(8,128)}, f32[58,1,256]{2,1,0:T(1,128)}, bf16[4,4,16,256]{3,2,1,0:T(8,128)(2,1)}) custom-call(bf16[8,256,256]{2,1,0:T(8,128)(2,1)} %get-tuple-element.12.gath, bf16[8,16,128]{2,1,0:T(8,128)(2,1)} %get-tuple-element.13.gathv, f32[8,128]{1,0:T(8,128)} %get-tuple-element.14.fac, ...), custom_call_target="tpu_custom_call" | custom-call | tf_op jit(solution)/shard_map/scale/pallas_call | solution.py:781

commit v6 on v5

--- a/solution.py
+++ b/solution.py
@@ -32,7 +32,7 @@
 
 def spans(nz):
     if nz == 16:
-        return ((13, 16), (10, 13), (7, 10), (4, 7), (0, 4)), ((0, 1), (1, 5), (5, 9), (9, 13), (13, 16))
+        return ((13, 16), (10, 13), (7, 10), (4, 7), (2, 4), (0, 2)), ((0, 1), (1, 5), (5, 9), (9, 13), (13, 16))
     return ((1, nz), (0, 1)), ((0, 1), (1, nz))
 
 

time: 78 us -> 77.5 us (level)
  no operation moved by 1% of the time
where the time goes in v6:
time: 77.5 us; the launch traced here: 76.7 us
  Pallas kernels  76.1 us (98%)
    pallas_call x1, Pallas kernels, per_device(): pl.pallas_call(functools.partial(relay_kernel, dims), out_shape=(jax.Shap...  73.3 us
    pallas_call x1, Pallas kernels, per_device(): pl.pallas_call(functools.partial(scale_kernel, nz), out_shape=(jax.ShapeD...  2.78 us

profile of v6, /device:TPU:6, one launch (start us, length us, event | category | flops | bytes accessed | tf_op | source)
XLA Modules:
  0.0 76.7 jit_solution(3936933913722019611)
XLA Ops:
  0.6 73.3 %relay.1 = (bf16[8,256,256]{2,1,0:T(8,128)(2,1)}, bf16[8,16,128]{2,1,0:T(8,128)(2,1)}, f32[8,128]{1,0:T(8,128)}, bf16[4,4,16,256]{3,2,1,0:T(8,128)(2,1)}) custom-call(bf16[4,4,16,256]{3,2,1,0:T(8,128)(2,1)} %bitcast.13, bf16[4,4,16,256]{3,2,1,0:T(8,128)(2,1)} %bitcast.14, bf16[256,1024]{1,0:T(8,128)(2,1)} %bitcast.11, bf16[1024,256]{1,0:T(8,128)(2,1)} %bitcast.12, ...), custom_call_target="tpu_custom_call" | custom-call | tf_op jit(solution)/shard_map/relay/pallas_call | solution.py:713
  73.9 2.8 %scale.1 = (f32[256,1024]{1,0:T(8,128)}, f32[1024,256]{1,0:T(8,128)}, f32[58,1,256]{2,1,0:T(1,128)}, bf16[4,4,16,256]{3,2,1,0:T(8,128)(2,1)}) custom-call(bf16[8,256,256]{2,1,0:T(8,128)(2,1)} %get-tuple-element.12.gath, bf16[8,16,128]{2,1,0:T(8,128)(2,1)} %get-tuple-element.13.gathv, f32[8,128]{1,0:T(8,128)} %get-tuple-element.14.fac, ...), custom_call_target="tpu_custom_call" | custom-call | tf_op jit(solution)/shard_map/scale/pallas_call | solution.py:781
